TPU v7x, 32 devices: a whole 2x2x4 slice. The times are simulated.
32 devices in a mesh: dp: 8 (over y, x, core), tensor: 4 (over z).
Axes of the slice: x: 2, y: 2, z: 4, core: 2. Of those that a mesh axis runs over, the one named last changes fastest.
Arguments:
- tokens: bfloat16 [512, 6144], P(('dp', 'tensor')), may hold values from -6 to 6
- router_weight: bfloat16 [6144, 8], replicated, may hold values from -0.078125 to 0.078125
- expert_ids: int32 [512, 2], P(('dp', 'tensor')), may hold values from 0 to 7, as said below
- gate_weight: bfloat16 [6144, 8192], P('dp', 'tensor'), may hold values from -0.078125 to 0.078125
- up_weight: bfloat16 [6144, 8192], P('dp', 'tensor'), may hold values from -0.078125 to 0.078125
Outputs:
- hidden: bfloat16 [512, 8192], P('dp', 'tensor')
Inputs may be any that keep to these rules, and one draw needn't show every extreme that they name: `expert_ids`: each row holds two different expert numbers; the share of tokens that name expert 0 varies from one index of dp to another.
All inputs are finite; a program needn't handle non-finite values.
Results may differ from a plain program's by a relative error of at most 0.0046.
Values may be sent and summed in bfloat16 or wider, within the bound.
A program may use at most 128 MiB of HBM per device.

v0:
```python
import jax
import jax.numpy as jnp
from jax import lax
from jax.sharding import PartitionSpec as P


def per_device(tokens, router_weight, expert_ids, gate_weight, up_weight):
    logits = jnp.dot(tokens, router_weight, preferred_element_type=jnp.float32)
    first_zero = expert_ids[:, 0] == 0
    routed = first_zero | (expert_ids[:, 1] == 0)
    other = jnp.where(first_zero, expert_ids[:, 1], expert_ids[:, 0])
    picked = jnp.arange(logits.shape[1], dtype=jnp.int32)[None, :] == other[:, None]
    other_logit = jnp.sum(jnp.where(picked, logits, jnp.float32(0.0)), axis=1)
    weight = jnp.where(routed, jax.nn.sigmoid(logits[:, 0] - other_logit), jnp.float32(0.0)).astype(
        jnp.bfloat16
    )
    rows, weights = (
        lax.all_gather(tokens, "tensor", axis=0, tiled=True),
        lax.all_gather(weight, "tensor", axis=0, tiled=True),
    )
    gate_part = jnp.dot(
        rows,
        lax.all_gather(gate_weight, "dp", axis=0, tiled=True),
        preferred_element_type=jnp.float32,
    )
    up_part = jnp.dot(
        rows,
        lax.all_gather(up_weight, "dp", axis=0, tiled=True),
        preferred_element_type=jnp.float32,
    )
    hidden = weights.astype(jnp.float32)[:, None] * jax.nn.silu(gate_part) * up_part
    return hidden.astype(jnp.bfloat16)


def solution(mesh):
    return jax.shard_map(
        per_device,
        mesh=mesh,
        in_specs=(
            P(("dp", "tensor"), None),
            P(),
            P(("dp", "tensor"), None),
            P("dp", "tensor"),
            P("dp", "tensor"),
        ),
        out_specs=P("dp", "tensor"),
        check_vma=False,
    )
```

profile of v0, /device:TPU:0, one launch (start us, length us, event | category | flops | bytes accessed | tf_op | source)
XLA Modules:
  0.0 282.7 jit_solution(10997266278550315734)
XLA Ops:
  6.5 0.0 copy-start
  6.5 0.0 all-gather.3.cloned.1.call-start
  6.5 0.7 all-gather.3.cloned.1.call-update
  7.3 0.0 all-gather.5.cloned.1.call-start
  7.3 0.7 all-gather.5.cloned.1.call-update
  8.0 1.2 dynamic-slice
  9.9 0.8 fusion.3
  10.7 0.0 copy-done
  10.7 1.1 select_reduce_fusion
  11.8 0.8 fusion.6
  12.6 0.2 dynamic-update-slice
  12.8 13.5 %all-reduce = bf16[64]{0:T(256)(128)(2,1)S(1)} all-reduce(bf16[64]{0:T(256)(128)(2,1)S(1)} %dynamic-update-slice), channel_id=1, replica_groups=mesh['dp'=8,'tensor'=4] {'tensor'}, use_global_device_ids=true, to_apply=%add | all-reduce | flops 64 | bytes 256
  26.3 16.7 %all_gather.13 = bf16[64,6144]{1,0:T(8,128)(2,1)S(1)} all-gather(bf16[16,6144]{1,0:T(8,128)(2,1)} %param.5), channel_id=1, replica_groups=mesh['dp'=8,'tensor'=4] {'tensor'}, dimensions={0}, use_global_device_ids=true | all-gather | bytes 983040 | tf_op jit(solution)/shard_map/all_gather | solution.py:18
  43.1 94.2 %all-gather.3.cloned.1.call-done = bf16[6144,2048]{1,0:T(8,128)(2,1)} async-done(((bf16[768,2048]{1,0:T(8,128)(2,1)}), bf16[6144,2048]{1,0:T(8,128)(2,1)}) %all-gather.3.cloned.1.call-update) | async-done | bytes 25165840 | tf_op jit(solution)/shard_map/all_gather | solution.py:23
  137.3 10.5 %fusion.7 = f32[64,2048]{1,0:T(8,128)S(1)} fusion(bf16[64,6144]{1,0:T(8,128)(2,1)S(1)} %all_gather.13, bf16[6144,2048]{1,0:T(8,128)(2,1)} %all-gather.3.cloned.1.call-done), kind=kOutput, calls=%fused_computation.13 | convolution fusion | flops 1610612736 | bytes 26476544 | tf_op jit(solution)/shard_map/dot_general | solution.py:21
  147.8 116.8 %all-gather.5.cloned.1.call-done = bf16[6144,2048]{1,0:T(8,128)(2,1)} async-done(((bf16[768,2048]{1,0:T(8,128)(2,1)}), bf16[6144,2048]{1,0:T(8,128)(2,1)}) %all-gather.5.cloned.1.call-update) | async-done | bytes 25165840 | tf_op jit(solution)/shard_map/all_gather | solution.py:28
  264.5 11.3 %fusion = bf16[64,2048]{1,0:T(8,128)(2,1)} fusion(bf16[64,6144]{1,0:T(8,128)(2,1)S(1)} %all_gather.13, bf16[6144,2048]{1,0:T(8,128)(2,1)} %all-gather.5.cloned.1.call-done, f32[64,2048]{1,0:T(8,128)S(1)} %fusion.7, f32[64]{0:T(128)S(1)} %convert_element_type.10), kind=kOutput, calls=%fused_computation.1 | convolution fusion | flops 1611530240 | bytes 26738944 | tf_op jit(solution)/shard_map/dot_general | solution.py:26
  (2 shorter events, 0.0 us)
Async XLA Ops:
  6.5 4.1 %copy-start = (bf16[6144,8]{0,1:T(8,128)(2,1)S(1)}, bf16[6144,8]{0,1:T(8,128)(2,1)}, u32[]{:S(2)}) copy-start(bf16[6144,8]{0,1:T(8,128)(2,1)} %param.6) | copy-start | bytes 294916
  6.5 130.8 %all-gather.3.cloned.1.call-start = ((), (), s32[]{:S(2)}) async-start(), calls=%async_computation | async-start | bytes 28311552 | tf_op jit(solution)/shard_map/all_gather | solution.py:23
  7.3 257.3 %all-gather.5.cloned.1.call-start = ((), (), s32[]{:S(2)}) async-start(), calls=%async_computation.1 | async-start | bytes 28311552 | tf_op jit(solution)/shard_map/all_gather | solution.py:28
Sparse Core Ops, SparseCore 0:
  9.2 128.0 all-gather.2
  139.2 125.3 all-gather.4
where the time goes:
time: 283 us
  waiting for transfers between devices  212 us (75%)
  blocking collectives  30.3 us (11%)
  matrix products  22.9 us (8%)
  between operations  14.1 us (5%)
    all_gather x1, waiting for transfers between devices, per_device(): lax.all_gather(up_weight, 'dp', axis=0, tiled=True)  117 us
    all_gather x1, waiting for transfers between devices, per_device(): lax.all_gather(gate_weight, 'dp', axis=0, tiled=True)  94.2 us
    all_gather x1, blocking collectives, per_device(): lax.all_gather(tokens, 'tensor', axis=0, tiled=True)  16.7 us
    unnamed x1, blocking collectives  13.5 us
    dot_general x1, matrix products, per_device(): jnp.dot(rows, lax.all_gather(up_weight, 'dp', axis=0, tiled=True), prefer...  11.3 us
    dot_general x1, matrix products, per_device(): jnp.dot(rows, lax.all_gather(gate_weight, 'dp', axis=0, tiled=True), pref...  10.5 us
  transfers between devices with their start and end apart: 2, of which 2 were waited for; matrix products, arithmetic and copies ran while one was open for 5% of the time, Pallas kernels for 0%

commit v1 on v0

v1 whole, which is shorter than its diff:
```python
import jax
import jax.numpy as jnp
from jax import lax
from jax.sharding import PartitionSpec as P


def share_of_expert(tokens, router_weight, expert_ids):
    logits = jnp.dot(tokens, router_weight, preferred_element_type=jnp.float32)
    first_zero = expert_ids[:, 0] == 0
    routed = first_zero | (expert_ids[:, 1] == 0)
    other = jnp.where(first_zero, expert_ids[:, 1], expert_ids[:, 0])
    picked = jnp.arange(logits.shape[1], dtype=jnp.int32)[None, :] == other[:, None]
    other_logit = jnp.sum(jnp.where(picked, logits, jnp.float32(0.0)), axis=1)
    return jnp.where(routed, jax.nn.sigmoid(logits[:, 0] - other_logit), jnp.float32(0.0)).astype(
        jnp.bfloat16
    )


def stationary_weights(mesh, tokens, router_weight, expert_ids, gate_weight, up_weight):
    dp, tensor = mesh.shape["dp"], mesh.shape["tensor"]
    rows, depth = tokens.shape[0], gate_weight.shape[0]
    weights = lax.all_gather(
        share_of_expert(tokens, router_weight, expert_ids), "tensor", axis=0, tiled=True
    )
    columns = lax.all_to_all(
        tokens.reshape(rows, dp, depth), "dp", split_axis=1, concat_axis=0, tiled=False
    )
    block = lax.all_gather(columns, "tensor", axis=1, tiled=True).reshape(dp * tensor * rows, depth)

    def summed(weight):
        part = jnp.dot(block, weight, preferred_element_type=jnp.float32).astype(jnp.bfloat16)
        part = part.reshape(dp, tensor * rows, -1)
        got = lax.all_to_all(part, "dp", split_axis=0, concat_axis=0, tiled=False)
        return jnp.sum(got.astype(jnp.float32), axis=0)

    gate, up = summed(gate_weight), summed(up_weight)
    hidden = weights.astype(jnp.float32)[:, None] * jax.nn.silu(gate) * up
    return hidden.astype(jnp.bfloat16)


def solution(mesh):
    def per_device(*args):
        return stationary_weights(mesh, *args)

    return jax.shard_map(
        per_device,
        mesh=mesh,
        in_specs=(
            P(("dp", "tensor"), None),
            P(),
            P(("dp", "tensor"), None),
            P("dp", "tensor"),
            P("dp", "tensor"),
        ),
        out_specs=P("dp", "tensor"),
        check_vma=False,
    )
```

time: 283 us -> 102 us (0.36)
  waiting for transfers between devices: 212 us -> 33.4 us
  matrix products: 22.9 us -> 8.58 us
  between operations: 14.1 us -> 0.78 us
  blocking collectives: 30.3 us -> 41.2 us
  starting transfers between devices: 0.04 us -> 8.67 us
  other arithmetic: 1.55 us -> 6.78 us
    all_gather x2 -> x0, waiting for transfers between devices: 211 us -> none  [the longest x1 117 us: per_device(): lax.all_gather(up_weight, 'dp', axis=0, tiled=True)]
    all_to_all x0 -> x2, waiting for transfers between devices: none -> 33.4 us  [summed(): got = lax.all_to_all(part, 'dp', split_axis=0, concat_axis=0, tiled=False)]
    dot_general x3, matrix products: 22.9 us -> 8.58 us  [the longest x2 8.4 us: summed(): jnp.dot(block, weight, preferred_element_type=jnp.float32)]
    all_to_all x0 -> x1, blocking collectives: none -> 11.2 us  [stationary_weights(): lax.all_to_all(tokens.reshape(rows, dp, depth), 'dp', split_axis=1, conca...]
    all_to_all x0 -> x2, starting transfers between devices: none -> 8.67 us  [summed(): got = lax.all_to_all(part, 'dp', split_axis=0, concat_axis=0, tiled=False)]
    reduce_sum x0 -> x2, other arithmetic: none -> 4.81 us  [summed(): return jnp.sum(got.astype(jnp.float32), axis=0)]
    unnamed x1, blocking collectives: 13.5 us -> 10 us
    all_gather x1, blocking collectives: 16.7 us -> 19.9 us  [stationary_weights(): lax.all_gather(columns, 'tensor', axis=1, tiled=True)]
  transfers between devices with their start and end apart: 2 -> 2, of which waited for: 2 -> 2; matrix products, arithmetic and copies ran while one was open for 5% -> 9% of each run, Pallas kernels for 0% -> 0%
where the time goes in v1:
time: 102 us
  blocking collectives  41.2 us (40%)
  waiting for transfers between devices  33.4 us (33%)
  starting transfers between devices  8.67 us (8%)
  matrix products  8.58 us (8%)
  other arithmetic  6.78 us (7%)
  local copies, waits for them, and re-layouts  2.2 us (2%)
    all_to_all x2, waiting for transfers between devices, summed(): got = lax.all_to_all(part, 'dp', split_axis=0, concat_axis=0, tiled=False)  33.4 us
    all_gather x1, blocking collectives, stationary_weights(): lax.all_gather(columns, 'tensor', axis=1, tiled=True)  19.9 us
    all_to_all x1, blocking collectives, stationary_weights(): lax.all_to_all(tokens.reshape(rows, dp, depth), 'dp', split_axis=1, conca...  11.2 us
    unnamed x1, blocking collectives  10 us
    all_to_all x2, starting transfers between devices, summed(): got = lax.all_to_all(part, 'dp', split_axis=0, concat_axis=0, tiled=False)  8.67 us
    dot_general x2, matrix products, summed(): jnp.dot(block, weight, preferred_element_type=jnp.float32)  8.4 us
    reduce_sum x2, other arithmetic, summed(): return jnp.sum(got.astype(jnp.float32), axis=0)  4.81 us
  transfers between devices with their start and end apart: 2, of which 2 were waited for; matrix products, arithmetic and copies ran while one was open for 9% of the time, Pallas kernels for 0%

profile of v1, /device:TPU:0, one launch (start us, length us, event | category | flops | bytes accessed | tf_op | source)
XLA Modules:
  0.0 101.6 jit_solution(9762511836838430949)
XLA Ops:
  0.0 0.0 copy-start
  0.0 1.1 %copy.10 = bf16[2,8,8,768]{3,2,1,0:T(8,128)(2,1)S(1)} copy(bf16[2,8,8,768]{3,1,2,0:T(8,128)(2,1)} %bitcast.38) | data formatting | bytes 393216
  1.2 11.2 %all_to_all.25 = bf16[1,16,8,768]{3,1,0,2:T(8,128)(2,1)S(1)} all-to-all(bf16[1,16,8,768]{3,1,0,2:T(8,128)(2,1)S(1)} %copy.7), channel_id=1, replica_groups=mesh['dp'=8,'tensor'=4] {'dp'}, dimensions={2} | all-to-all | bytes 393216 | tf_op jit(solution)/shard_map/all_to_all | solution.py:25
  12.4 0.1 copy.8
  12.4 19.9 %all-gather = bf16[8,1,64,1,768]{4,0,3,1,2:T(8,128)(2,1)S(1)} all-gather(bf16[8,1,16,1,768]{4,0,3,1,2:T(8,128)(2,1)S(1)} %copy.8), channel_id=2, replica_groups=mesh['dp'=8,'tensor'=4] {'tensor'}, dimensions={2}, use_global_device_ids=true | all-gather | bytes 983040 | tf_op jit(solution)/shard_map/all_gather | solution.py:28
  32.4 0.1 copy.9
  32.5 0.0 copy-start.1
  32.5 0.0 copy-done
  32.5 3.2 %convolution_convert_fusion = bf16[512,2048]{1,0:T(8,128)(2,1)} fusion(bf16[512,768]{1,0:T(8,128)(2,1)S(1)} %bitcast.36, bf16[768,2048]{1,0:T(8,128)(2,1)S(1)} %copy-done), kind=kOutput, calls=%fused_computation.2 | convolution fusion | flops 1611661312 | bytes 6029312 | tf_op jit(solution)/shard_map/dot_general | solution.py:31
  35.7 0.0 copy-done.1
  35.7 4.3 %all-to-all-start.2 = ((bf16[8,64,2048]{2,1,0:T(8,128)(2,1)}), bf16[8,64,2048]{2,1,0:T(8,128)(2,1)}, u32[]{:S(2)}, u32[]{:S(2)}) async-start(bf16[8,64,2048]{2,1,0:T(8,128)(2,1)} %bitcast.35), calls=%async_computation.2 | async-start | bytes 4194304 | tf_op jit(solution)/shard_map/all_to_all | solution.py:33
  40.0 5.2 %convolution_convert_fusion.1 = bf16[512,2048]{1,0:T(8,128)(2,1)} fusion(bf16[512,768]{1,0:T(8,128)(2,1)} %bitcast.37, bf16[768,2048]{1,0:T(8,128)(2,1)} %param.8), kind=kOutput, calls=%fused_computation.3 | convolution fusion | flops 1611661312 | bytes 6029312 | tf_op jit(solution)/shard_map/dot_general | solution.py:31
  45.3 0.0 copy-start.5
  45.3 0.0 copy-start.4
  45.3 0.0 copy-start.2
  45.3 0.0 copy-start.3
  45.3 21.4 %all-to-all-done.2 = bf16[8,64,2048]{2,1,0:T(8,128)(2,1)} async-done(((bf16[8,64,2048]{2,1,0:T(8,128)(2,1)}), bf16[8,64,2048]{2,1,0:T(8,128)(2,1)}, u32[]{:S(2)}, u32[]{:S(2)}) %all-to-all-start.2) | async-done | bytes 2097184 | tf_op jit(solution)/shard_map/all_to_all | solution.py:33
  66.7 4.3 %all-to-all-start.1 = ((bf16[8,64,2048]{2,1,0:T(8,128)(2,1)}), bf16[8,64,2048]{2,1,0:T(8,128)(2,1)}, u32[]{:S(2)}, u32[]{:S(2)}) async-start(bf16[8,64,2048]{2,1,0:T(8,128)(2,1)} %bitcast.34), calls=%async_computation.1 | async-start | bytes 4194304 | tf_op jit(solution)/shard_map/all_to_all | solution.py:33
  71.0 0.0 copy-done.5
  71.0 0.6 dynamic-slice
  72.3 0.0 copy-done.4
  72.3 0.0 copy-done.2
  72.3 0.0 copy-done.3
  72.3 0.2 select_reduce_fusion
  72.5 0.2 dynamic-update-slice
  72.8 10.0 %all-reduce = bf16[64]{0:T(256)(128)(2,1)S(1)} all-reduce(bf16[64]{0:T(256)(128)(2,1)S(1)} %dynamic-update-slice), channel_id=1, replica_groups=mesh['dp'=8,'tensor'=4] {'tensor'}, use_global_device_ids=true, to_apply=%add | all-reduce | flops 64 | bytes 256
  82.8 2.8 %convert_reduce_fusion = f32[64,2048]{1,0:T(8,128)} fusion(bf16[8,64,2048]{2,1,0:T(8,128)(2,1)} %all-to-all-done.2), kind=kLoop, calls=%fused_computation | loop fusion | flops 1966080 | bytes 2621440 | tf_op jit(solution)/shard_map/reduce_sum | solution.py:34
  85.6 12.0 %all-to-all-done.1 = bf16[8,64,2048]{2,1,0:T(8,128)(2,1)} async-done(((bf16[8,64,2048]{2,1,0:T(8,128)(2,1)}), bf16[8,64,2048]{2,1,0:T(8,128)(2,1)}, u32[]{:S(2)}, u32[]{:S(2)}) %all-to-all-start.1) | async-done | bytes 2097184 | tf_op jit(solution)/shard_map/all_to_all | solution.py:33
  97.7 2.0 %convert_reduce_fusion.1 = f32[64,2048]{1,0:T(8,128)S(1)} fusion(bf16[8,64,2048]{2,1,0:T(8,128)(2,1)} %all-to-all-done.1), kind=kLoop, calls=%fused_computation.1 | loop fusion | flops 1966080 | bytes 2621440 | tf_op jit(solution)/shard_map/reduce_sum | solution.py:34
  99.7 1.9 %multiply_convert_fusion = bf16[64,2048]{1,0:T(8,128)(2,1)} fusion(f32[64,2048]{1,0:T(8,128)} %convert_reduce_fusion, f32[64,2048]{1,0:T(8,128)S(1)} %convert_reduce_fusion.1, f32[64]{0:T(128)S(1)} %convert_element_type.22), kind=kLoop, calls=%fused_computation.4 | loop fusion | flops 917504 | bytes 1310976 | tf_op jit(solution)/shard_map/convert_element_type | solution.py:38
  (5 shorter events, 0.1 us)
Async XLA Ops:
  0.0 32.5 %copy-start = (bf16[768,2048]{1,0:T(8,128)(2,1)S(1)}, bf16[768,2048]{1,0:T(8,128)(2,1)}, u32[]{:S(2)}) copy-start(bf16[768,2048]{1,0:T(8,128)(2,1)} %param.9) | copy-start | bytes 9437188
  32.5 3.2 %copy-start.1 = (bf16[8,1,64,1,768]{4,2,0,3,1:T(8,128)(2,1)}, bf16[8,1,64,1,768]{4,2,0,3,1:T(8,128)(2,1)S(1)}, u32[]{:S(2)}) copy-start(bf16[8,1,64,1,768]{4,2,0,3,1:T(8,128)(2,1)S(1)} %copy.9) | copy-start | bytes 2359300
  35.7 31.0 %all-to-all-start.2 = ((bf16[8,64,2048]{2,1,0:T(8,128)(2,1)}), bf16[8,64,2048]{2,1,0:T(8,128)(2,1)}, u32[]{:S(2)}, u32[]{:S(2)}) async-start(bf16[8,64,2048]{2,1,0:T(8,128)(2,1)} %bitcast.35), calls=%async_computation.2 | async-start | bytes 4194304 | tf_op jit(solution)/shard_map/all_to_all | solution.py:33
  45.3 25.8 %copy-start.5 = (u32[32]{0:T(128)S(1)}, u32[32]{0:T(128)}, u32[]{:S(2)}) copy-start(u32[32]{0:T(128)} %constant.12) | copy-start | bytes 388
  45.3 27.0 %copy-start.4 = (s32[16,2]{0,1:T(2,128)S(1)}, s32[16,2]{0,1:T(2,128)}, u32[]{:S(2)}) copy-start(s32[16,2]{0,1:T(2,128)} %param.7) | copy-start | bytes 388
  45.3 27.0 %copy-start.2 = (bf16[16,6144]{1,0:T(8,128)(2,1)S(1)}, bf16[16,6144]{1,0:T(8,128)(2,1)}, u32[]{:S(2)}) copy-start(bf16[16,6144]{1,0:T(8,128)(2,1)} %param.5) | copy-start | bytes 589828
  45.3 27.0 %copy-start.3 = (bf16[6144,8]{0,1:T(8,128)(2,1)S(1)}, bf16[6144,8]{0,1:T(8,128)(2,1)}, u32[]{:S(2)}) copy-start(bf16[6144,8]{0,1:T(8,128)(2,1)} %param.6) | copy-start | bytes 294916
  66.7 31.0 %all-to-all-start.1 = ((bf16[8,64,2048]{2,1,0:T(8,128)(2,1)}), bf16[8,64,2048]{2,1,0:T(8,128)(2,1)}, u32[]{:S(2)}, u32[]{:S(2)}) async-start(bf16[8,64,2048]{2,1,0:T(8,128)(2,1)} %bitcast.34), calls=%async_computation.1 | async-start | bytes 4194304 | tf_op jit(solution)/shard_map/all_to_all | solution.py:33

commit v2 on v1

--- a/solution.py
+++ b/solution.py
@@ -1,7 +1,14 @@
+import functools
+
 import jax
 import jax.numpy as jnp
 from jax import lax
+from jax.experimental import pallas as pl
+from jax.experimental.pallas import tpu as pltpu
 from jax.sharding import PartitionSpec as P
+
+MESH = pl.DeviceIdType.MESH
+TILE = 512
 
 
 def share_of_expert(tokens, router_weight, expert_ids):
@@ -38,9 +45,338 @@
     return hidden.astype(jnp.bfloat16)
 
 
+def order_of_planes(n):
+    return [sorted(range(n), key=lambda other: (abs(other - plane), other)) for plane in range(n)]
+
+
+def kernel(
+    n,
+    tok_ref,
+    router_ref,
+    ids_ref,
+    gate_ref,
+    up_ref,
+    out_ref,
+    w_buf,
+    x_buf,
+    share_buf,
+    share_all,
+    keep1,
+    send1,
+    recv1,
+    keep2,
+    send2,
+    recv2,
+    keep3,
+    send3,
+    recv3,
+    load_sem,
+    a_send,
+    a_recv,
+    z_up,
+    z_down,
+    z_recv,
+    s_send,
+    s_recv,
+    c1_send,
+    c1_recv,
+    c2_send,
+    c2_recv,
+    c3_send,
+    c3_recv,
+):
+    rows = tok_ref.shape[0]
+    depth, width = gate_ref.shape
+    me, plane = lax.axis_index("dp"), lax.axis_index("tensor")
+    bits = [lax.rem(lax.div(me, m), 2) for m in (1, 2, 4)]
+
+    def partner(mask):
+        found = me
+        for b, m in enumerate((1, 2, 4)):
+            if mask & m:
+                found = found + m * (1 - 2 * bits[b])
+        return found
+
+    def slot_of(mask):
+        return (mask & 1) * 4 + (mask & 2) + (mask >> 2)
+
+    loads = [
+        pltpu.make_async_copy(ref, w_buf.at[i], load_sem.at[i])
+        for i, ref in enumerate((gate_ref, up_ref))
+    ]
+    for load in loads:
+        load.start()
+
+    barrier = pltpu.get_barrier_semaphore()
+    for mask in range(1, 8):
+        pl.semaphore_signal(barrier, inc=1, device_id=(partner(mask), plane), device_id_type=MESH)
+    for hop in range(1, n):
+        pl.semaphore_signal(
+            barrier, inc=1, device_id=(me, lax.rem(plane + hop, n)), device_id_type=MESH
+        )
+    pl.semaphore_wait(barrier, 7 + n - 1)
+
+    spread = []
+    for mask in (6, 4, 2, 7, 5, 3, 1):
+        to = partner(mask)
+        spread.append(
+            pltpu.make_async_remote_copy(
+                src_ref=tok_ref.at[:, pl.ds(pl.multiple_of(to * depth, depth), depth)],
+                dst_ref=x_buf.at[plane, pl.ds(slot_of(mask) * rows, rows), :],
+                send_sem=a_send.at[mask],
+                recv_sem=a_recv.at[mask],
+                device_id=(to, plane),
+                device_id_type=MESH,
+            )
+        )
+    for copy in spread:
+        copy.start()
+    x_buf[plane, 0:rows, :] = tok_ref[:, pl.ds(pl.multiple_of(me * depth, depth), depth)]
+
+    def along(source, step, sem):
+        return pltpu.make_async_remote_copy(
+            src_ref=x_buf.at[source],
+            dst_ref=x_buf.at[source],
+            send_sem=sem.at[source],
+            recv_sem=z_recv.at[source],
+            device_id=(me, plane + step),
+            device_id_type=MESH,
+        )
+
+    for copy in spread:
+        copy.wait_recv()
+
+    @pl.when(plane < n - 1)
+    def _():
+        along(plane, 1, z_up).start()
+
+    @pl.when(plane > 0)
+    def _():
+        along(plane, -1, z_down).start()
+
+    logits = lax.dot_general(
+        router_ref[...],
+        tok_ref[...],
+        (((1,), (1,)), ((), ())),
+        preferred_element_type=jnp.float32,
+    )
+    ids = ids_ref[...]
+    first, second = ids[0:1, :], ids[1:2, :]
+    routed = (first == 0) | (second == 0)
+    other = jnp.where(first == 0, second, first)
+    picked = lax.broadcasted_iota(jnp.int32, logits.shape, 0) == other
+    other_logit = jnp.sum(jnp.where(picked, logits, 0.0), axis=0, keepdims=True)
+    share = jnp.where(routed, jax.nn.sigmoid(logits[0:1, :] - other_logit), 0.0)
+    square = (rows, rows)
+    own = lax.broadcasted_iota(jnp.int32, square, 0) == lax.broadcasted_iota(jnp.int32, square, 1)
+    column = jnp.sum(jnp.where(own, jnp.broadcast_to(share, square), 0.0), axis=1, keepdims=True)
+    spread_share = jnp.broadcast_to(column, share_buf.shape).astype(share_buf.dtype)
+    share_buf[...] = spread_share
+    share_all[plane] = spread_share
+    shares = [
+        pltpu.make_async_remote_copy(
+            src_ref=share_buf,
+            dst_ref=share_all.at[plane],
+            send_sem=s_send.at[hop],
+            recv_sem=s_recv.at[hop],
+            device_id=(me, lax.rem(plane + hop, n)),
+            device_id_type=MESH,
+        )
+        for hop in range(1, n)
+    ]
+    for copy in shares:
+        copy.start()
+
+    table = order_of_planes(n)
+
+    def source_of(k):
+        found = plane
+        for p in range(n):
+            found = jnp.where(plane == p, table[p][k], found)
+        return found
+
+    def exchange(src, dst, send_sem, recv_sem, k, w, mask):
+        return pltpu.make_async_remote_copy(
+            src_ref=src.at[k, w],
+            dst_ref=dst.at[k, w],
+            send_sem=send_sem.at[k, w],
+            recv_sem=recv_sem.at[k, w],
+            device_id=(partner(mask), plane),
+            device_id_type=MESH,
+        )
+
+    def over_core(k, w):
+        return exchange(send1, recv1, c1_send, c1_recv, k, w, 1)
+
+    def over_first(k, w):
+        return exchange(send2, recv2, c2_send, c2_recv, k, w, (2, 4)[w])
+
+    def over_second(k, w):
+        return exchange(send3, recv3, c3_send, c3_recv, k, w, (4, 2)[w])
+
+    tile = min(TILE, width)
+
+    def multiply(k):
+        source = source_of(k)
+        for w in range(2):
+            if k == 0:
+                loads[w].wait()
+
+            @pl.loop(0, width // tile)
+            def _(i):
+                columns = pl.ds(pl.multiple_of(i * tile, tile), tile)
+                part = jnp.dot(
+                    x_buf[source], w_buf[w, :, columns], preferred_element_type=jnp.float32
+                )
+                keep1[k, w, :, columns] = part[: 4 * rows]
+                send1[k, w, :, columns] = part[4 * rows :]
+
+            over_core(k, w).start()
+
+    def after_core(k):
+        for w in range(2):
+            over_core(k, w).wait_recv()
+            for xb in range(2):
+                for yb in range(2):
+                    at = pl.ds((xb * 2 + yb) * rows, rows)
+                    total = keep1[k, w, at, :] + recv1[k, w, at, :]
+                    leaves, place = ((xb, yb), (yb, xb))[w]
+                    to = pl.ds(place * rows, rows)
+                    if leaves:
+                        send2[k, w, to, :] = total.astype(send2.dtype)
+                    else:
+                        keep2[k, w, to, :] = total
+            over_first(k, w).start()
+
+    def after_first(k):
+        for w in range(2):
+            over_first(k, w).wait_recv()
+            leave, stay = pl.ds(rows, rows), pl.ds(0, rows)
+            send3[k, w] = (
+                keep2[k, w, leave, :] + recv2[k, w, leave, :].astype(jnp.float32)
+            ).astype(send3.dtype)
+            over_second(k, w).start()
+            keep3[k, w] = keep2[k, w, stay, :] + recv2[k, w, stay, :].astype(jnp.float32)
+
+    def finish(k):
+        source = source_of(k)
+        for w in range(2):
+            over_second(k, w).wait_recv()
+        gate = keep3[k, 0] + recv3[k, 0].astype(jnp.float32)
+        up = keep3[k, 1] + recv3[k, 1].astype(jnp.float32)
+        part = share_all[source][:, 0:1].astype(jnp.float32)
+        hidden = part * (gate * jax.nn.sigmoid(gate)) * up
+        out_ref[pl.ds(pl.multiple_of(source * rows, rows), rows), :] = hidden.astype(out_ref.dtype)
+
+    for k in range(n):
+        if k:
+
+            @pl.when(plane - k >= 0)
+            def _():
+                along(plane - k, 1, z_up).wait_recv()
+
+            @pl.when((plane - k >= 0) & (plane < n - 1))
+            def _():
+                along(plane - k, 1, z_up).start()
+
+            @pl.when(plane + k < n)
+            def _():
+                along(plane + k, -1, z_down).wait_recv()
+
+            @pl.when((plane + k < n) & (plane > 0))
+            def _():
+                along(plane + k, -1, z_down).start()
+
+        multiply(k)
+        if k >= 1:
+            after_first(k - 1)
+        after_core(k)
+        if k == 2:
+            for copy in shares:
+                copy.wait_recv()
+        if k >= 2:
+            finish(k - 2)
+    after_first(n - 1)
+    finish(n - 2)
+    finish(n - 1)
+
+    for copy in spread + shares:
+        copy.wait_send()
+    for p in range(n):
+
+        @pl.when((plane >= p) & (plane < n - 1))
+        def _():
+            along(p, 1, z_up).wait_send()
+
+        @pl.when((plane <= p) & (plane > 0))
+        def _():
+            along(p, -1, z_down).wait_send()
+
+    for k in range(n):
+        for w in range(2):
+            over_core(k, w).wait_send()
+            over_first(k, w).wait_send()
+            over_second(k, w).wait_send()
+
+
+def one_kernel(mesh, tokens, router_weight, expert_ids, gate_weight, up_weight):
+    n = mesh.shape["tensor"]
+    rows = tokens.shape[0]
+    depth, width = gate_weight.shape
+    f32, bf16 = jnp.float32, jnp.bfloat16
+    dma = pltpu.SemaphoreType.DMA
+    vmem = pl.BlockSpec(memory_space=pltpu.VMEM)
+    hbm = pl.BlockSpec(memory_space=pl.ANY)
+    return pl.pallas_call(
+        functools.partial(kernel, n),
+        out_shape=jax.ShapeDtypeStruct((n * rows, width), bf16),
+        in_specs=[vmem, vmem, vmem, hbm, hbm],
+        out_specs=vmem,
+        scratch_shapes=[
+            pltpu.VMEM((2, depth, width), bf16),
+            pltpu.VMEM((n, 8 * rows, depth), bf16),
+            pltpu.VMEM((rows, 128), bf16),
+            pltpu.VMEM((n, rows, 128), bf16),
+            pltpu.VMEM((n, 2, 4 * rows, width), f32),
+            pltpu.VMEM((n, 2, 4 * rows, width), f32),
+            pltpu.VMEM((n, 2, 4 * rows, width), f32),
+            pltpu.VMEM((n, 2, 2 * rows, width), f32),
+            pltpu.VMEM((n, 2, 2 * rows, width), bf16),
+            pltpu.VMEM((n, 2, 2 * rows, width), bf16),
+            pltpu.VMEM((n, 2, rows, width), f32),
+            pltpu.VMEM((n, 2, rows, width), bf16),
+            pltpu.VMEM((n, 2, rows, width), bf16),
+            dma((2,)),
+            dma((8,)),
+            dma((8,)),
+            dma((n,)),
+            dma((n,)),
+            dma((n,)),
+            dma((n,)),
+            dma((n,)),
+            dma((n, 2)),
+            dma((n, 2)),
+            dma((n, 2)),
+            dma((n, 2)),
+            dma((n, 2)),
+            dma((n, 2)),
+        ],
+        compiler_params=pltpu.CompilerParams(
+            collective_id=0, has_side_effects=True, vmem_limit_bytes=58 * 2**20
+        ),
+        cost_estimate=pl.CostEstimate(
+            flops=2 * n * 8 * rows * depth * 2 * width,
+            bytes_accessed=2 * depth * width * 2,
+            transcendentals=n * rows * width,
+        ),
+    )(tokens, router_weight.T, expert_ids.T, gate_weight, up_weight)
+
+
 def solution(mesh):
+    chosen = one_kernel if mesh.shape["dp"] == 8 and mesh.shape["tensor"] == 4 else stationary_weights
+
     def per_device(*args):
-        return stationary_weights(mesh, *args)
+        return chosen(mesh, *args)
 
     return jax.shard_map(
         per_device,

time: 102 us -> 44.1 us (0.43)
  Pallas kernels: 0 us -> 42.3 us
  blocking collectives: 41.2 us -> 0 us
  waiting for transfers between devices: 33.4 us -> 0 us
  starting transfers between devices: 8.67 us -> 0 us
  matrix products: 8.58 us -> 0 us
  other arithmetic: 6.78 us -> 0 us
    pallas_call x0 -> x1, Pallas kernels: none -> 42.3 us  [one_kernel(): pl.pallas_call(functools.partial(kernel, n), out_shape=jax.ShapeDtypeStru...]
    all_to_all x2 -> x0, waiting for transfers between devices: 33.4 us -> none  [summed(): got = lax.all_to_all(part, 'dp', split_axis=0, concat_axis=0, tiled=False)]
    all_gather x1 -> x0, blocking collectives: 19.9 us -> none  [stationary_weights(): lax.all_gather(columns, 'tensor', axis=1, tiled=True)]
    all_to_all x1 -> x0, blocking collectives: 11.2 us -> none  [stationary_weights(): lax.all_to_all(tokens.reshape(rows, dp, depth), 'dp', split_axis=1, conca...]
    unnamed x1 -> x0, blocking collectives: 10 us -> none
    all_to_all x2 -> x0, starting transfers between devices: 8.67 us -> none  [summed(): got = lax.all_to_all(part, 'dp', split_axis=0, concat_axis=0, tiled=False)]
    dot_general x3 -> x0, matrix products: 8.58 us -> none  [the longest x2 8.4 us: summed(): jnp.dot(block, weight, preferred_element_type=jnp.float32)]
    reduce_sum x2 -> x0, other arithmetic: 4.81 us -> none  [summed(): return jnp.sum(got.astype(jnp.float32), axis=0)]
  transfers between devices with their start and end apart: 2 -> 0, of which waited for: 2 -> 0; matrix products, arithmetic and copies ran while one was open for 9% -> 0% of each run, Pallas kernels for 0% -> 0%
where the time goes in v2:
time: 44.1 us; the launch traced here: 44 us
  Pallas kernels  42.3 us (96%)
  local copies, waits for them, and re-layouts  1.67 us (4%)
    pallas_call x1, Pallas kernels, one_kernel(): pl.pallas_call(functools.partial(kernel, n), out_shape=jax.ShapeDtypeStru...  42.3 us
    unnamed x1, local copies, waits for them, and re-layouts  1.67 us

profile of v2, /device:TPU:0, one launch (start us, length us, event | category | flops | bytes accessed | tf_op | source)
XLA Modules:
  0.0 44.0 jit_solution(8381896479930051009)
XLA Ops:
  0.0 42.3 %shard_map.55 = bf16[64,2048]{1,0:T(8,128)(2,1)} custom-call(bf16[16,6144]{1,0:T(8,128)(2,1)} %tok_ref.1, bf16[8,6144]{1,0:T(8,128)(2,1)} %bitcast.2, s32[2,16]{1,0:T(2,128)} %bitcast.3, bf16[768,2048]{1,0:T(8,128)(2,1)} %gate_ref.1, bf16[768,2048]{1,0:T(8,128)(2,1)} %up_ref.1), custom_call_target="tpu_custom_call" | custom-call | flops 3221225472 | bytes 6291456 | tf_op jit(solution)/shard_map/pallas_call | solution.py:330
  42.3 1.7 %copy.7 = bf16[64,2048]{1,0:T(8,128)(2,1)} copy(bf16[64,2048]{1,0:T(8,128)(2,1)} %shard_map.55) | data formatting | bytes 524288

commit v3 on v2

--- a/solution.py
+++ b/solution.py
@@ -57,6 +57,8 @@
     gate_ref,
     up_ref,
     out_ref,
+    tok_buf,
+    router_buf,
     w_buf,
     x_buf,
     share_buf,
@@ -100,12 +102,23 @@
     def slot_of(mask):
         return (mask & 1) * 4 + (mask & 2) + (mask >> 2)
 
+    def columns_of(device):
+        return tok_ref.at[:, pl.ds(pl.multiple_of(device * depth, depth), depth)]
+
     loads = [
-        pltpu.make_async_copy(ref, w_buf.at[i], load_sem.at[i])
-        for i, ref in enumerate((gate_ref, up_ref))
+        pltpu.make_async_copy(src, dst, load_sem.at[i])
+        for i, (src, dst) in enumerate(
+            (
+                (gate_ref, w_buf.at[0]),
+                (up_ref, w_buf.at[1]),
+                (tok_ref, tok_buf),
+                (router_ref, router_buf),
+                (columns_of(me), x_buf.at[plane, pl.ds(0, rows), :]),
+            )
+        )
     ]
-    for load in loads:
-        load.start()
+    for i in (4, 2, 3, 0, 1):
+        loads[i].start()
 
     barrier = pltpu.get_barrier_semaphore()
     for mask in range(1, 8):
@@ -121,7 +134,7 @@
         to = partner(mask)
         spread.append(
             pltpu.make_async_remote_copy(
-                src_ref=tok_ref.at[:, pl.ds(pl.multiple_of(to * depth, depth), depth)],
+                src_ref=columns_of(to),
                 dst_ref=x_buf.at[plane, pl.ds(slot_of(mask) * rows, rows), :],
                 send_sem=a_send.at[mask],
                 recv_sem=a_recv.at[mask],
@@ -131,32 +144,56 @@
         )
     for copy in spread:
         copy.start()
-    x_buf[plane, 0:rows, :] = tok_ref[:, pl.ds(pl.multiple_of(me * depth, depth), depth)]
-
-    def along(source, step, sem):
+
+    def along(source, half, step, sem):
+        part = pl.ds(half * 4 * rows, 4 * rows)
         return pltpu.make_async_remote_copy(
-            src_ref=x_buf.at[source],
-            dst_ref=x_buf.at[source],
-            send_sem=sem.at[source],
-            recv_sem=z_recv.at[source],
+            src_ref=x_buf.at[source, part, :],
+            dst_ref=x_buf.at[source, part, :],
+            send_sem=sem.at[source, half],
+            recv_sem=z_recv.at[source, half],
             device_id=(me, plane + step),
             device_id_type=MESH,
         )
 
-    for copy in spread:
-        copy.wait_recv()
-
-    @pl.when(plane < n - 1)
-    def _():
-        along(plane, 1, z_up).start()
-
-    @pl.when(plane > 0)
-    def _():
-        along(plane, -1, z_down).start()
-
+    loads[4].wait()
+    for half in range(2):
+        for copy in spread[3 * half : 3 + 4 * half]:
+            copy.wait_recv()
+
+        @pl.when(plane < n - 1)
+        def _():
+            along(plane, half, 1, z_up).start()
+
+        @pl.when(plane > 0)
+        def _():
+            along(plane, half, -1, z_down).start()
+
+    def pass_on(k, half):
+        @pl.when((plane - k >= 0) & (plane < n - 1))
+        def _():
+            along(plane - k, half, 1, z_up).wait_recv()
+            along(plane - k, half, 1, z_up).start()
+
+        @pl.when((plane + k < n) & (plane > 0))
+        def _():
+            along(plane + k, half, -1, z_down).wait_recv()
+            along(plane + k, half, -1, z_down).start()
+
+    def take(k, half):
+        @pl.when((plane - k >= 0) & (plane == n - 1))
+        def _():
+            along(plane - k, half, 1, z_up).wait_recv()
+
+        @pl.when((plane + k < n) & (plane == 0))
+        def _():
+            along(plane + k, half, -1, z_down).wait_recv()
+
+    loads[2].wait()
+    loads[3].wait()
     logits = lax.dot_general(
-        router_ref[...],
-        tok_ref[...],
+        router_buf[...],
+        tok_buf[...],
         (((1,), (1,)), ((), ())),
         preferred_element_type=jnp.float32,
     )
@@ -270,33 +307,23 @@
 
     for k in range(n):
         if k:
-
-            @pl.when(plane - k >= 0)
-            def _():
-                along(plane - k, 1, z_up).wait_recv()
-
-            @pl.when((plane - k >= 0) & (plane < n - 1))
-            def _():
-                along(plane - k, 1, z_up).start()
-
-            @pl.when(plane + k < n)
-            def _():
-                along(plane + k, -1, z_down).wait_recv()
-
-            @pl.when((plane + k < n) & (plane > 0))
-            def _():
-                along(plane + k, -1, z_down).start()
-
+            pass_on(k, 1)
+            take(k, 0)
+            take(k, 1)
         multiply(k)
-        if k >= 1:
-            after_first(k - 1)
+        if k + 1 < n:
+            pass_on(k + 1, 0)
+        if k >= 2:
+            after_first(k - 2)
         after_core(k)
-        if k == 2:
-            for copy in shares:
-                copy.wait_recv()
-        if k >= 2:
-            finish(k - 2)
-    after_first(n - 1)
+    for copy in shares:
+        copy.wait_recv()
+    for k in range(n):
+        if k >= n - 2:
+            after_first(k)
+        if k == n - 2:
+            for done in range(n - 2):
+                finish(done)
     finish(n - 2)
     finish(n - 1)
 
@@ -306,11 +333,13 @@
 
         @pl.when((plane >= p) & (plane < n - 1))
         def _():
-            along(p, 1, z_up).wait_send()
+            for half in range(2):
+                along(p, half, 1, z_up).wait_send()
 
         @pl.when((plane <= p) & (plane > 0))
         def _():
-            along(p, -1, z_down).wait_send()
+            for half in range(2):
+                along(p, half, -1, z_down).wait_send()
 
     for k in range(n):
         for w in range(2):
@@ -330,9 +359,11 @@
     return pl.pallas_call(
         functools.partial(kernel, n),
         out_shape=jax.ShapeDtypeStruct((n * rows, width), bf16),
-        in_specs=[vmem, vmem, vmem, hbm, hbm],
+        in_specs=[hbm, hbm, vmem, hbm, hbm],
         out_specs=vmem,
         scratch_shapes=[
+            pltpu.VMEM(tokens.shape, bf16),
+            pltpu.VMEM(router_weight.shape[::-1], bf16),
             pltpu.VMEM((2, depth, width), bf16),
             pltpu.VMEM((n, 8 * rows, depth), bf16),
             pltpu.VMEM((rows, 128), bf16),
@@ -346,14 +377,14 @@
             pltpu.VMEM((n, 2, rows, width), f32),
             pltpu.VMEM((n, 2, rows, width), bf16),
             pltpu.VMEM((n, 2, rows, width), bf16),
-            dma((2,)),
+            dma((5,)),
             dma((8,)),
             dma((8,)),
+            dma((n, 2)),
+            dma((n, 2)),
+            dma((n, 2)),
             dma((n,)),
             dma((n,)),
-            dma((n,)),
-            dma((n,)),
-            dma((n,)),
             dma((n, 2)),
             dma((n, 2)),
             dma((n, 2)),
@@ -362,7 +393,7 @@
             dma((n, 2)),
         ],
         compiler_params=pltpu.CompilerParams(
-            collective_id=0, has_side_effects=True, vmem_limit_bytes=58 * 2**20
+            collective_id=0, has_side_effects=True, vmem_limit_bytes=63_300_000
         ),
         cost_estimate=pl.CostEstimate(
             flops=2 * n * 8 * rows * depth * 2 * width,

time: 44.1 us -> 40.4 us (0.916)
  Pallas kernels: 42.3 us -> 38.6 us
    pallas_call x1, Pallas kernels: 42.3 us -> 38.6 us  [one_kernel(): pl.pallas_call(functools.partial(kernel, n), out_shape=jax.ShapeDtypeStru...]
where the time goes in v3:
time: 40.4 us; the launch traced here: 40.2 us
  Pallas kernels  38.6 us (96%)
  local copies, waits for them, and re-layouts  1.67 us (4%)
    pallas_call x1, Pallas kernels, one_kernel(): pl.pallas_call(functools.partial(kernel, n), out_shape=jax.ShapeDtypeStru...  38.6 us
    unnamed x1, local copies, waits for them, and re-layouts  1.67 us

profile of v3, /device:TPU:0, one launch (start us, length us, event | category | flops | bytes accessed | tf_op | source)
XLA Modules:
  0.0 40.2 jit_solution(7770310024014505241)
XLA Ops:
  0.0 38.6 %shard_map.55 = bf16[64,2048]{1,0:T(8,128)(2,1)} custom-call(bf16[16,6144]{1,0:T(8,128)(2,1)} %tok_ref.1, bf16[8,6144]{1,0:T(8,128)(2,1)} %bitcast.2, s32[2,16]{1,0:T(2,128)} %bitcast.3, bf16[768,2048]{1,0:T(8,128)(2,1)} %gate_ref.1, bf16[768,2048]{1,0:T(8,128)(2,1)} %up_ref.1), custom_call_target="tpu_custom_call" | custom-call | flops 3221225472 | bytes 6291456 | tf_op jit(solution)/shard_map/pallas_call | solution.py:359
  38.6 1.7 %copy.7 = bf16[64,2048]{1,0:T(8,128)(2,1)} copy(bf16[64,2048]{1,0:T(8,128)(2,1)} %shard_map.55) | data formatting | bytes 524288

commit v4 on v3

--- a/solution.py
+++ b/solution.py
@@ -8,7 +8,7 @@
 from jax.sharding import PartitionSpec as P
 
 MESH = pl.DeviceIdType.MESH
-TILE = 512
+PARTS = 2
 
 
 def share_of_expert(tokens, router_weight, expert_ids):
@@ -246,38 +246,35 @@
         return exchange(send1, recv1, c1_send, c1_recv, k, w, 1)
 
     def over_first(k, w):
-        return exchange(send2, recv2, c2_send, c2_recv, k, w, (2, 4)[w])
+        return exchange(send2, recv2, c2_send, c2_recv, k, w, (2, 4)[w % 2])
 
     def over_second(k, w):
-        return exchange(send3, recv3, c3_send, c3_recv, k, w, (4, 2)[w])
-
-    tile = min(TILE, width)
+        return exchange(send3, recv3, c3_send, c3_recv, k, w, (4, 2)[w % 2])
+
+    tile = width // PARTS
+    units = 2 * PARTS
 
     def multiply(k):
         source = source_of(k)
-        for w in range(2):
-            if k == 0:
+        for w in range(units):
+            if k == 0 and w < 2:
                 loads[w].wait()
-
-            @pl.loop(0, width // tile)
-            def _(i):
-                columns = pl.ds(pl.multiple_of(i * tile, tile), tile)
-                part = jnp.dot(
-                    x_buf[source], w_buf[w, :, columns], preferred_element_type=jnp.float32
-                )
-                keep1[k, w, :, columns] = part[: 4 * rows]
-                send1[k, w, :, columns] = part[4 * rows :]
-
+            columns = pl.ds(w // 2 * tile, tile)
+            part = jnp.dot(
+                x_buf[source], w_buf[w % 2, :, columns], preferred_element_type=jnp.float32
+            )
+            keep1[k, w] = part[: 4 * rows]
+            send1[k, w] = part[4 * rows :]
             over_core(k, w).start()
 
     def after_core(k):
-        for w in range(2):
+        for w in range(units):
             over_core(k, w).wait_recv()
             for xb in range(2):
                 for yb in range(2):
                     at = pl.ds((xb * 2 + yb) * rows, rows)
                     total = keep1[k, w, at, :] + recv1[k, w, at, :]
-                    leaves, place = ((xb, yb), (yb, xb))[w]
+                    leaves, place = ((xb, yb), (yb, xb))[w % 2]
                     to = pl.ds(place * rows, rows)
                     if leaves:
                         send2[k, w, to, :] = total.astype(send2.dtype)
@@ -286,7 +283,7 @@
             over_first(k, w).start()
 
     def after_first(k):
-        for w in range(2):
+        for w in range(units):
             over_first(k, w).wait_recv()
             leave, stay = pl.ds(rows, rows), pl.ds(0, rows)
             send3[k, w] = (
@@ -297,13 +294,16 @@
 
     def finish(k):
         source = source_of(k)
-        for w in range(2):
+        for w in range(0, units, 2):
             over_second(k, w).wait_recv()
-        gate = keep3[k, 0] + recv3[k, 0].astype(jnp.float32)
-        up = keep3[k, 1] + recv3[k, 1].astype(jnp.float32)
-        part = share_all[source][:, 0:1].astype(jnp.float32)
-        hidden = part * (gate * jax.nn.sigmoid(gate)) * up
-        out_ref[pl.ds(pl.multiple_of(source * rows, rows), rows), :] = hidden.astype(out_ref.dtype)
+            over_second(k, w + 1).wait_recv()
+            gate = keep3[k, w] + recv3[k, w].astype(jnp.float32)
+            up = keep3[k, w + 1] + recv3[k, w + 1].astype(jnp.float32)
+            share_of_row = share_all[source][:, 0:1].astype(jnp.float32)
+            hidden = share_of_row * (gate * jax.nn.sigmoid(gate)) * up
+            out_ref[
+                pl.ds(pl.multiple_of(source * rows, rows), rows), pl.ds(w // 2 * tile, tile)
+            ] = hidden.astype(out_ref.dtype)
 
     for k in range(n):
         if k:
@@ -313,13 +313,13 @@
         multiply(k)
         if k + 1 < n:
             pass_on(k + 1, 0)
-        if k >= 2:
-            after_first(k - 2)
         after_core(k)
+        if k >= 1:
+            after_first(k - 1)
     for copy in shares:
         copy.wait_recv()
     for k in range(n):
-        if k >= n - 2:
+        if k >= n - 1:
             after_first(k)
         if k == n - 2:
             for done in range(n - 2):
@@ -342,7 +342,7 @@
                 along(p, half, -1, z_down).wait_send()
 
     for k in range(n):
-        for w in range(2):
+        for w in range(units):
             over_core(k, w).wait_send()
             over_first(k, w).wait_send()
             over_second(k, w).wait_send()
@@ -368,15 +368,15 @@
             pltpu.VMEM((n, 8 * rows, depth), bf16),
             pltpu.VMEM((rows, 128), bf16),
             pltpu.VMEM((n, rows, 128), bf16),
-            pltpu.VMEM((n, 2, 4 * rows, width), f32),
-            pltpu.VMEM((n, 2, 4 * rows, width), f32),
-            pltpu.VMEM((n, 2, 4 * rows, width), f32),
-            pltpu.VMEM((n, 2, 2 * rows, width), f32),
-            pltpu.VMEM((n, 2, 2 * rows, width), bf16),
-            pltpu.VMEM((n, 2, 2 * rows, width), bf16),
-            pltpu.VMEM((n, 2, rows, width), f32),
-            pltpu.VMEM((n, 2, rows, width), bf16),
-            pltpu.VMEM((n, 2, rows, width), bf16),
+            pltpu.VMEM((n, 2 * PARTS, 4 * rows, width // PARTS), f32),
+            pltpu.VMEM((n, 2 * PARTS, 4 * rows, width // PARTS), f32),
+            pltpu.VMEM((n, 2 * PARTS, 4 * rows, width // PARTS), f32),
+            pltpu.VMEM((n, 2 * PARTS, 2 * rows, width // PARTS), f32),
+            pltpu.VMEM((n, 2 * PARTS, 2 * rows, width // PARTS), bf16),
+            pltpu.VMEM((n, 2 * PARTS, 2 * rows, width // PARTS), bf16),
+            pltpu.VMEM((n, 2 * PARTS, rows, width // PARTS), f32),
+            pltpu.VMEM((n, 2 * PARTS, rows, width // PARTS), bf16),
+            pltpu.VMEM((n, 2 * PARTS, rows, width // PARTS), bf16),
             dma((5,)),
             dma((8,)),
             dma((8,)),
@@ -385,12 +385,12 @@
             dma((n, 2)),
             dma((n,)),
             dma((n,)),
-            dma((n, 2)),
-            dma((n, 2)),
-            dma((n, 2)),
-            dma((n, 2)),
-            dma((n, 2)),
-            dma((n, 2)),
+            dma((n, 2 * PARTS)),
+            dma((n, 2 * PARTS)),
+            dma((n, 2 * PARTS)),
+            dma((n, 2 * PARTS)),
+            dma((n, 2 * PARTS)),
+            dma((n, 2 * PARTS)),
         ],
         compiler_params=pltpu.CompilerParams(
             collective_id=0, has_side_effects=True, vmem_limit_bytes=63_300_000

time: 40.4 us -> 38.8 us (0.960)
  Pallas kernels: 38.6 us -> 36.9 us
    pallas_call x1, Pallas kernels: 38.6 us -> 36.9 us  [one_kernel(): pl.pallas_call(functools.partial(kernel, n), out_shape=jax.ShapeDtypeStru...]
where the time goes in v4:
time: 38.8 us; the launch traced here: 38.6 us
  Pallas kernels  36.9 us (95%)
  local copies, waits for them, and re-layouts  1.67 us (4%)
    pallas_call x1, Pallas kernels, one_kernel(): pl.pallas_call(functools.partial(kernel, n), out_shape=jax.ShapeDtypeStru...  36.9 us
    unnamed x1, local copies, waits for them, and re-layouts  1.67 us

profile of v4, /device:TPU:0, one launch (start us, length us, event | category | flops | bytes accessed | tf_op | source)
XLA Modules:
  0.0 38.6 jit_solution(6961673537063451807)
XLA Ops:
  0.0 36.9 %shard_map.55 = bf16[64,2048]{1,0:T(8,128)(2,1)} custom-call(bf16[16,6144]{1,0:T(8,128)(2,1)} %tok_ref.1, bf16[8,6144]{1,0:T(8,128)(2,1)} %bitcast.2, s32[2,16]{1,0:T(2,128)} %bitcast.3, bf16[768,2048]{1,0:T(8,128)(2,1)} %gate_ref.1, bf16[768,2048]{1,0:T(8,128)(2,1)} %up_ref.1), custom_call_target="tpu_custom_call" | custom-call | flops 3221225472 | bytes 6291456 | tf_op jit(solution)/shard_map/pallas_call | solution.py:359
  36.9 1.7 %copy.7 = bf16[64,2048]{1,0:T(8,128)(2,1)} copy(bf16[64,2048]{1,0:T(8,128)(2,1)} %shard_map.55) | data formatting | bytes 524288
